TPU v7x, 32 devices: a whole 2x2x4 slice. The times are simulated.
32 devices in a mesh: gx: 2 (over y), gy: 4 (over x, core), gz: 4 (over z).
Axes of the slice: x: 2, y: 2, z: 4, core: 2. Of those that a mesh axis runs over, the one named last changes fastest.
Arguments:
- right_side: float32 [2, 4, 4, 64, 512], P('gx', 'gy', 'gz'), may hold values from -6 to 6
- diag_blocks: float32 [4, 64, 64], replicated, may hold values from -0.27 to 17.9, as said below
- face_blocks: float32 [6, 4, 64, 64], replicated, may hold values from -2.42 to 0.22
- prolong: float32 [8, 64, 64], replicated, may hold values from -0.75 to 0.75
- mats_fine: int32 [2, 4, 4, 512], P('gx', 'gy', 'gz'), may hold values from 0 to 3
- mats_mid: int32 [2, 4, 4, 64], P('gx', 'gy', 'gz'), may hold values from 0 to 3
- mats_coarse: int32 [2, 4, 4, 8], P('gx', 'gy', 'gz'), may hold values from 0 to 3
Outputs:
- solution: float32 [2, 4, 4, 64, 512], P('gx', 'gy', 'gz')
Inputs may be any that keep to these rules, and one draw needn't show every extreme that they name: `diag_blocks`: each block is symmetric positive definite.
All inputs are finite; a program needn't handle non-finite values.
Results may differ from a plain program's by a relative error of at most 0.0003.
Values sent between devices are 32-bit elements; how exact they have to be, the bound alone decides.
No kernel may reach another device: no remote copies, remote signals or barrier semaphores. Data moves between devices by JAX's collectives and lax.ppermute only.
A program may use at most 64 MiB of HBM per device.

v0:
```python
from functools import partial

import jax
import jax.numpy as jnp
from jax import lax
from jax.sharding import PartitionSpec as P

MODES = 64
MATERIALS = 4
SWEEPS = 2
COARSE_SWEEPS = 4
CYCLES = 2
CX = 8
CY = 8
CZ = 8


relax_weight = 0.7
restrict_scale = 0.6
highest = lax.Precision.HIGHEST


def padded_2(shard, sides, width):
    for axis, dim in sides:
        size, length = (lax.axis_size(axis), shard.shape[dim])
        up = [(i, (i + 1) % size) for i in range(size - 1)]
        down = [(j, i) for i, j in up]
        last = lax.slice_in_dim(shard, length - width, length, axis=dim)
        first = lax.slice_in_dim(shard, 0, width, axis=dim)
        before = lax.ppermute(last, axis, up)
        after = lax.ppermute(first, axis, down)
        shard = jnp.concatenate([before, shard, after], axis=dim)
    return shard


def inverse_blocks(diag_blocks):
    identity = jnp.eye(MODES, dtype=diag_blocks.dtype)
    result = []
    for material in range(MATERIALS):
        factor = jnp.linalg.cholesky(diag_blocks[material])
        result.append(jax.scipy.linalg.cho_solve((factor, True), identity))
    return jnp.stack(result).reshape(MATERIALS * MODES, MODES)


def coupling_matrix(diag_blocks, face_blocks):
    blocks = jnp.concatenate([diag_blocks[None], face_blocks], axis=0)
    return jnp.transpose(blocks, (1, 2, 0, 3)).reshape(MATERIALS * MODES, 7 * MODES)


def choose_blocks(weights, columns, onehot):
    product = jnp.dot(weights, columns, precision=highest, preferred_element_type=jnp.float32)
    product = product.reshape(MATERIALS, MODES, columns.shape[1])
    return jnp.sum(product * onehot.reshape(MATERIALS, 1, columns.shape[1]), axis=0)


def operate(padded, onehot, coupling):
    centre = padded[:, 1:-1, 1:-1, 1:-1]
    stacked = jnp.concatenate(
        [
            centre,
            padded[:, 2:, 1:-1, 1:-1],
            padded[:, :-2, 1:-1, 1:-1],
            padded[:, 1:-1, 2:, 1:-1],
            padded[:, 1:-1, :-2, 1:-1],
            padded[:, 1:-1, 1:-1, 2:],
            padded[:, 1:-1, 1:-1, :-2],
        ],
        axis=0,
    )
    columns = stacked.reshape(7 * MODES, -1)
    return choose_blocks(coupling, columns, onehot.reshape(MATERIALS, -1)).reshape(centre.shape)


def apply_inverse(inverse, field, onehot):
    return choose_blocks(inverse, field.reshape(MODES, -1), onehot.reshape(MATERIALS, -1)).reshape(
        field.shape
    )


def restrict(field, prolong):
    blocked = field.reshape(
        MODES, field.shape[1] // 2, 2, field.shape[2] // 2, 2, field.shape[3] // 2, 2
    )
    return restrict_scale * jnp.einsum(
        "abcji,jxaybzc->ixyz", prolong.reshape(2, 2, 2, MODES, MODES), blocked, precision=highest
    )


def expand(coarse_field, prolong):
    finer = jnp.einsum(
        "abcji,ixyz->jxaybzc",
        prolong.reshape(2, 2, 2, MODES, MODES),
        coarse_field,
        precision=highest,
    )
    return finer.reshape(
        MODES, 2 * coarse_field.shape[1], 2 * coarse_field.shape[2], 2 * coarse_field.shape[3]
    )


def make_onehot(materials):
    return (materials[None] == jnp.arange(MATERIALS, dtype=jnp.int32)[:, None, None, None]).astype(
        jnp.float32
    )


def fine_border(field):
    return padded_2(field, (("gx", 1), ("gy", 2), ("gz", 3)), 1)


def section_border(field):
    padded = padded_2(field, (("gx", 1), ("gy", 2)), 1)
    return jnp.pad(padded, ((0, 0), (0, 0), (0, 0), (1, 1)))


def smooth(iterate, source, onehot, border, inverse, coupling):
    residual = source - operate(border(iterate), onehot, coupling)
    return iterate + relax_weight * apply_inverse(inverse, residual, onehot)


def coarse_solve(source, onehot, border, inverse, coupling):
    iterate = relax_weight * apply_inverse(inverse, source, onehot)
    for repeat in range(COARSE_SWEEPS - 1):
        iterate = smooth(iterate, source, onehot, border, inverse, coupling)
    return iterate


def middle_cycle(source, onehot, border, inverse, coupling, prolong, coarse_solver):
    iterate = relax_weight * apply_inverse(inverse, source, onehot)
    iterate = smooth(iterate, source, onehot, border, inverse, coupling)
    residual = source - operate(border(iterate), onehot, coupling)
    iterate = iterate + expand(coarse_solver(restrict(residual, prolong)), prolong)
    for repeat in range(SWEEPS):
        iterate = smooth(iterate, source, onehot, border, inverse, coupling)
    return iterate


def single_steps(iterate, actions, source, onehot, inverse, coupling):
    residual = None
    for action in actions:
        if action == "sweep":
            iterate = smooth(iterate, source, onehot, fine_border, inverse, coupling)
        else:
            residual = source - operate(fine_border(iterate), onehot, coupling)
    return (iterate, residual)


def per_device(right_side, diag_blocks, face_blocks, prolong, mats_fine, mats_mid, mats_coarse):
    inverse = inverse_blocks(diag_blocks)
    coupling = coupling_matrix(diag_blocks, face_blocks)
    source = right_side[0, 0, 0].reshape(MODES, CX, CY, CZ)
    onehot_fine = make_onehot(mats_fine[0, 0, 0].reshape(CX, CY, CZ))
    onehot_mid = make_onehot(mats_mid[0, 0, 0].reshape(CX // 2, CY // 2, CZ // 2))
    onehot_coarse = make_onehot(mats_coarse[0, 0, 0].reshape(CX // 4, CY // 4, CZ // 4))
    stepper = partial(
        single_steps, source=source, onehot=onehot_fine, inverse=inverse, coupling=coupling
    )
    iterate = relax_weight * apply_inverse(inverse, source, onehot_fine)
    for cycle_index in range(CYCLES):
        if cycle_index == 0:
            actions = ["sweep"] * (SWEEPS - 1) + ["residual"]
        else:
            actions = ["sweep"] * SWEEPS + ["residual"]
        iterate, residual = stepper(iterate, actions)
        gathered_source = lax.all_gather(restrict(residual, prolong), "gz", axis=3, tiled=True)
        gathered_mid = lax.all_gather(onehot_mid, "gz", axis=3, tiled=True)
        gathered_coarse = lax.all_gather(onehot_coarse, "gz", axis=3, tiled=True)
        local_solver = partial(
            coarse_solve,
            onehot=gathered_coarse,
            border=section_border,
            inverse=inverse,
            coupling=coupling,
        )
        section_field = middle_cycle(
            gathered_source, gathered_mid, section_border, inverse, coupling, prolong, local_solver
        )
        iterate = iterate + expand(
            lax.dynamic_slice_in_dim(section_field, lax.axis_index("gz") * (CZ // 2), CZ // 2, 3),
            prolong,
        )
        iterate, unused_residual = stepper(iterate, ["sweep"] * SWEEPS)
    return iterate.reshape(MODES, CX * CY * CZ)[None, None, None]


def solution(mesh):
    placed = (
        P("gx", "gy", "gz", None, None),
        P(),
        P(),
        P(),
        P("gx", "gy", "gz", None),
        P("gx", "gy", "gz", None),
        P("gx", "gy", "gz", None),
    )
    return jax.shard_map(
        per_device,
        mesh=mesh,
        in_specs=placed,
        out_specs=P("gx", "gy", "gz", None, None),
        check_vma=False,
    )
```

profile of v0, /device:TPU:0, one launch (start us, length us, event | category | flops | bytes accessed | tf_op | source)
XLA Modules:
  0.0 594.0 jit_solution(17117302072970611200)
XLA Ops:
  2.5 5.8 cholesky.74
  9.7 4.9 custom-call.10
  14.6 5.9 cholesky.85
  21.8 4.9 custom-call.11
  26.7 5.9 cholesky.96
  33.9 4.9 custom-call.12
  38.8 5.9 cholesky.107
  46.0 4.9 custom-call.13
  54.2 4.9 collective-permute-start.1
  60.7 4.2 collective-permute-done
  71.1 3.5 collective-permute-start.5
  76.4 4.2 collective-permute-done.4
  89.2 3.4 collective-permute-done.6
  96.2 13.7 %all_gather.15 = f32[4,4,4,16]{2,1,0,3:T(4,128)S(1)} all-gather(f32[4,4,4,4]{2,1,0,3:T(4,128)S(1)} %fusion.98), channel_id=1, replica_groups=mesh['gx'=2,'gy'=4,'gz'=4] {'gz'}, dimensions={3}, use_global_device_ids=true | all-gather | bytes 5120 | tf_op jit(solution)/shard_map/all_gather | solution.py:166
  113.5 4.3 collective-permute-done.10
  122.3 13.5 %all_gather.14 = f32[64,4,4,16]{0,2,1,3:T(4,128)S(1)} all-gather(f32[64,4,4,4]{0,2,1,3:T(4,128)S(1)} %copy.170), channel_id=1, replica_groups=mesh['gx'=2,'gy'=4,'gz'=4] {'gz'}, dimensions={3}, use_global_device_ids=true | all-gather | bytes 81920 | tf_op jit(solution)/shard_map/all_gather | solution.py:165
  140.3 4.2 collective-permute-done.12
  147.1 6.0 %collective-permute-done.14 = f32[64,6,1,16]{0,3,2,1:T(8,128)S(1)} collective-permute-done((f32[64,6,1,16]{0,3,2,1:T(8,128)S(1)}, f32[64,6,1,16]{0,3,2,1:T(8,128)S(1)}, u32[]{:S(2)}, u32[]{:S(2)}) %collective-permute-start.14) | collective-permute-done | bytes 24608 | tf_op jit(solution)/shard_map/ppermute | solution.py:31
  158.7 3.6 collective-permute-done.16
  162.3 3.3 collective-permute-start.19
  167.0 13.1 %all_gather.16 = f32[4,2,2,8]{0,2,1,3:T(2,128)S(1)} all-gather(f32[4,2,2,2]{0,2,1,3:T(2,128)S(1)} %compare_convert_fusion), channel_id=1, replica_groups=mesh['gx'=2,'gy'=4,'gz'=4] {'gz'}, dimensions={3}, use_global_device_ids=true | all-gather | bytes 640 | tf_op jit(solution)/shard_map/all_gather | solution.py:167
  185.6 4.2 collective-permute-done.20
  192.4 5.4 collective-permute-done.22
  202.3 4.2 collective-permute-done.24
  218.0 4.2 collective-permute-done.28
  234.8 4.2 collective-permute-done.32
  239.1 3.0 collective-permute-start.35
  251.1 4.2 collective-permute-done.36
  255.3 3.3 collective-permute-start.39
  268.6 4.2 collective-permute-done.40
  272.9 3.3 collective-permute-start.43
  283.7 4.3 collective-permute-done.44
  296.4 4.6 collective-permute-done.46
  304.3 3.6 collective-permute-done.48
  307.9 3.2 collective-permute-start.51
  312.9 4.3 collective-permute-done.50
  325.5 4.6 collective-permute-done.52
  333.5 3.6 collective-permute-done.54
  337.1 3.5 collective-permute-start.57
  342.4 4.3 collective-permute-done.56
  355.0 4.6 collective-permute-done.58
  362.9 3.6 collective-permute-done.60
  370.3 4.3 collective-permute-done.62
  382.9 4.6 collective-permute-done.64
  390.8 3.6 collective-permute-done.66
  398.1 4.3 collective-permute-done.68
  407.1 13.4 %all_gather.17 = f32[64,4,4,16]{0,2,1,3:T(4,128)S(1)} all-gather(f32[64,4,4,4]{0,2,1,3:T(4,128)S(1)} %copy.212), channel_id=1, replica_groups=mesh['gx'=2,'gy'=4,'gz'=4] {'gz'}, dimensions={3}, use_global_device_ids=true | all-gather | bytes 81920 | tf_op jit(solution)/shard_map/all_gather | solution.py:165
  424.3 4.2 collective-permute-done.70
  431.2 4.6 collective-permute-done.72
  440.7 4.2 collective-permute-done.74
  444.9 3.3 collective-permute-start.77
  457.2 4.2 collective-permute-done.78
  461.4 3.3 collective-permute-start.81
  473.2 4.2 collective-permute-done.82
  488.9 4.2 collective-permute-done.86
  505.8 4.2 collective-permute-done.90
  522.0 4.2 collective-permute-done.94
  526.3 3.3 collective-permute-start.97
  539.6 4.2 collective-permute-done.98
  543.8 3.3 collective-permute-start.101
  554.2 4.3 collective-permute-done.102
  566.9 4.3 collective-permute-done.104
  578.4 3.7 collective-permute-start.109
  583.9 4.3 collective-permute-done.108
  (543 shorter events, 283.6 us)
Async XLA Ops:
  54.2 6.5 %collective-permute-start.1 = (f32[64,1,8,8]{0,3,2,1:T(8,128)S(1)}, f32[64,1,8,8]{0,3,2,1:T(8,128)S(1)}, u32[]{:S(2)}, u32[]{:S(2)}) collective-permute-start(f32[64,1,8,8]{0,3,2,1:T(8,128)S(1)} %get-tuple-element.129), channel_id=1, source_target_pairs={{0,16},{1,17},{2,18},{3,19},{4,20},{5,21},{6,22},{7,23},{8,24},{9,... | collective-permute-start | bytes 49160 | tf_op jit(solution)/shard_map/ppermute | solution.py:30
  59.1 5.8 collective-permute-start
  66.2 4.8 collective-permute-start.2
  71.1 5.3 collective-permute-start.5
  74.6 6.0 %collective-permute-start.4 = (f32[64,10,10,1]{0,3,2,1:T(1,128)S(1)}, f32[64,10,10,1]{0,3,2,1:T(1,128)S(1)}, u32[]{:S(2)}, u32[]{:S(2)}) collective-permute-start(f32[64,10,10,1]{0,3,2,1:T(1,128)S(1)} %get-tuple-element.58), channel_id=1, source_target_pairs={{1,0},{2,1},{3,2},{5,4},{6,5},{7,6},{9,8},{10,9},{11,10},{13,12},{... | collective-permute-start | bytes 76808 | tf_op jit(solution)/shard_map/ppermute | solution.py:31
  84.9 4.3 collective-permute-start.7
  86.5 6.1 %collective-permute-start.6 = (f32[64,1,8,8]{0,3,2,1:T(8,128)S(1)}, f32[64,1,8,8]{0,3,2,1:T(8,128)S(1)}, u32[]{:S(2)}, u32[]{:S(2)}) collective-permute-start(f32[64,1,8,8]{0,3,2,1:T(8,128)S(1)} %get-tuple-element.128), channel_id=1, source_target_pairs={{16,0},{17,1},{18,2},{19,3},{20,4},{21,5},{22,6},{23,7},{24,8},{25... | collective-permute-start | bytes 49160 | tf_op jit(solution)/shard_map/ppermute | solution.py:31
  92.7 17.5 %collective-permute-start.9 = (f32[64,10,1,8]{0,3,2,1:T(8,128)S(1)}, f32[64,10,1,8]{0,3,2,1:T(8,128)S(1)}, u32[]{:S(2)}, u32[]{:S(2)}) collective-permute-start(f32[64,10,1,8]{0,3,2,1:T(8,128)S(1)} %get-tuple-element.82), channel_id=1, source_target_pairs={{0,4},{4,8},{8,12},{1,5},{5,9},{9,13},{2,6},{6,10},{10,14},{3,7},{... | collective-permute-start | bytes 61448 | tf_op jit(solution)/shard_map/ppermute | solution.py:30
  94.7 15.4 %collective-permute-start.8 = (f32[64,10,1,8]{0,3,2,1:T(8,128)S(1)}, f32[64,10,1,8]{0,3,2,1:T(8,128)S(1)}, u32[]{:S(2)}, u32[]{:S(2)}) collective-permute-start(f32[64,10,1,8]{0,3,2,1:T(8,128)S(1)} %get-tuple-element.83), channel_id=1, source_target_pairs={{4,0},{8,4},{12,8},{5,1},{9,5},{13,9},{6,2},{10,6},{14,10},{7,3},{... | collective-permute-start | bytes 61448 | tf_op jit(solution)/shard_map/ppermute | solution.py:31
  111.7 6.0 %collective-permute-start.10 = (f32[64,10,10,1]{0,3,2,1:T(1,128)S(1)}, f32[64,10,10,1]{0,3,2,1:T(1,128)S(1)}, u32[]{:S(2)}, u32[]{:S(2)}) collective-permute-start(f32[64,10,10,1]{0,3,2,1:T(1,128)S(1)} %get-tuple-element.54), channel_id=1, source_target_pairs={{1,0},{2,1},{3,2},{5,4},{6,5},{7,6},{9,8},{10,9},{11,10},{13,12},{... | collective-permute-start | bytes 76808 | tf_op jit(solution)/shard_map/ppermute | solution.py:31
  138.7 5.8 collective-permute-start.12
  145.8 7.3 %collective-permute-start.14 = (f32[64,6,1,16]{0,3,2,1:T(8,128)S(1)}, f32[64,6,1,16]{0,3,2,1:T(8,128)S(1)}, u32[]{:S(2)}, u32[]{:S(2)}) collective-permute-start(f32[64,6,1,16]{0,3,2,1:T(8,128)S(1)} %get-tuple-element.162), channel_id=1, source_target_pairs={{4,0},{8,4},{12,8},{5,1},{9,5},{13,9},{6,2},{10,6},{14,10},{7,3},{... | collective-permute-start | bytes 73736 | tf_op jit(solution)/shard_map/ppermute | solution.py:31
  156.5 5.8 collective-permute-start.16
  162.3 18.0 %collective-permute-start.19 = (f32[64,6,1,16]{0,3,2,1:T(8,128)S(1)}, f32[64,6,1,16]{0,3,2,1:T(8,128)S(1)}, u32[]{:S(2)}, u32[]{:S(2)}) collective-permute-start(f32[64,6,1,16]{0,3,2,1:T(8,128)S(1)} %get-tuple-element.157), channel_id=1, source_target_pairs={{0,4},{4,8},{8,12},{1,5},{5,9},{9,13},{2,6},{6,10},{10,14},{3,7},{... | collective-permute-start | bytes 73736 | tf_op jit(solution)/shard_map/ppermute | solution.py:30
  165.6 14.7 %collective-permute-start.18 = (f32[64,6,1,16]{0,3,2,1:T(8,128)S(1)}, f32[64,6,1,16]{0,3,2,1:T(8,128)S(1)}, u32[]{:S(2)}, u32[]{:S(2)}) collective-permute-start(f32[64,6,1,16]{0,3,2,1:T(8,128)S(1)} %get-tuple-element.158), channel_id=1, source_target_pairs={{4,0},{8,4},{12,8},{5,1},{9,5},{13,9},{6,2},{10,6},{14,10},{7,3},{... | collective-permute-start | bytes 73736 | tf_op jit(solution)/shard_map/ppermute | solution.py:31
  184.2 5.5 collective-permute-start.20
  191.1 6.7 %collective-permute-start.22 = (f32[64,4,1,8]{0,3,2,1:T(8,128)S(1)}, f32[64,4,1,8]{0,3,2,1:T(8,128)S(1)}, u32[]{:S(2)}, u32[]{:S(2)}) collective-permute-start(f32[64,4,1,8]{0,3,2,1:T(8,128)S(1)} %get-tuple-element.238), channel_id=1, source_target_pairs={{4,0},{8,4},{12,8},{5,1},{9,5},{13,9},{6,2},{10,6},{14,10},{7,3},{... | collective-permute-start | bytes 24584 | tf_op jit(solution)/shard_map/ppermute | solution.py:31
  200.9 5.5 collective-permute-start.24
  206.5 4.3 collective-permute-start.27
  216.6 5.5 collective-permute-start.28
  222.2 4.4 collective-permute-start.31
  233.3 5.8 collective-permute-start.32
  239.1 4.3 collective-permute-start.35
  249.5 5.8 collective-permute-start.36
  255.3 4.6 collective-permute-start.39
  267.0 5.8 collective-permute-start.40
  272.9 4.6 collective-permute-start.43
  282.0 6.0 %collective-permute-start.44 = (f32[64,10,10,1]{0,3,2,1:T(1,128)S(1)}, f32[64,10,10,1]{0,3,2,1:T(1,128)S(1)}, u32[]{:S(2)}, u32[]{:S(2)}) collective-permute-start(f32[64,10,10,1]{0,3,2,1:T(1,128)S(1)} %get-tuple-element.50), channel_id=1, source_target_pairs={{1,0},{2,1},{3,2},{5,4},{6,5},{7,6},{9,8},{10,9},{11,10},{13,12},{... | collective-permute-start | bytes 76808 | tf_op jit(solution)/shard_map/ppermute | solution.py:31
  294.8 6.1 %collective-permute-start.46 = (f32[64,1,8,8]{0,3,2,1:T(8,128)S(1)}, f32[64,1,8,8]{0,3,2,1:T(8,128)S(1)}, u32[]{:S(2)}, u32[]{:S(2)}) collective-permute-start(f32[64,1,8,8]{0,3,2,1:T(8,128)S(1)} %get-tuple-element.124), channel_id=1, source_target_pairs={{16,0},{17,1},{18,2},{19,3},{20,4},{21,5},{22,6},{23,7},{24,8},{25... | collective-permute-start | bytes 49160 | tf_op jit(solution)/shard_map/ppermute | solution.py:31
  303.0 4.9 collective-permute-start.48
  307.9 5.0 collective-permute-start.51
  311.2 6.0 %collective-permute-start.50 = (f32[64,10,10,1]{0,3,2,1:T(1,128)S(1)}, f32[64,10,10,1]{0,3,2,1:T(1,128)S(1)}, u32[]{:S(2)}, u32[]{:S(2)}) collective-permute-start(f32[64,10,10,1]{0,3,2,1:T(1,128)S(1)} %get-tuple-element.46), channel_id=1, source_target_pairs={{1,0},{2,1},{3,2},{5,4},{6,5},{7,6},{9,8},{10,9},{11,10},{13,12},{... | collective-permute-start | bytes 76808 | tf_op jit(solution)/shard_map/ppermute | solution.py:31
  324.0 6.1 %collective-permute-start.52 = (f32[64,1,8,8]{0,3,2,1:T(8,128)S(1)}, f32[64,1,8,8]{0,3,2,1:T(8,128)S(1)}, u32[]{:S(2)}, u32[]{:S(2)}) collective-permute-start(f32[64,1,8,8]{0,3,2,1:T(8,128)S(1)} %get-tuple-element.122), channel_id=1, source_target_pairs={{16,0},{17,1},{18,2},{19,3},{20,4},{21,5},{22,6},{23,7},{24,8},{25... | collective-permute-start | bytes 49160 | tf_op jit(solution)/shard_map/ppermute | solution.py:31
  332.1 4.9 collective-permute-start.54
  337.1 5.3 collective-permute-start.57
  340.6 6.0 %collective-permute-start.56 = (f32[64,10,10,1]{0,3,2,1:T(1,128)S(1)}, f32[64,10,10,1]{0,3,2,1:T(1,128)S(1)}, u32[]{:S(2)}, u32[]{:S(2)}) collective-permute-start(f32[64,10,10,1]{0,3,2,1:T(1,128)S(1)} %get-tuple-element.42), channel_id=1, source_target_pairs={{1,0},{2,1},{3,2},{5,4},{6,5},{7,6},{9,8},{10,9},{11,10},{13,12},{... | collective-permute-start | bytes 76808 | tf_op jit(solution)/shard_map/ppermute | solution.py:31
  353.5 6.1 %collective-permute-start.58 = (f32[64,1,8,8]{0,3,2,1:T(8,128)S(1)}, f32[64,1,8,8]{0,3,2,1:T(8,128)S(1)}, u32[]{:S(2)}, u32[]{:S(2)}) collective-permute-start(f32[64,1,8,8]{0,3,2,1:T(8,128)S(1)} %get-tuple-element.120), channel_id=1, source_target_pairs={{16,0},{17,1},{18,2},{19,3},{20,4},{21,5},{22,6},{23,7},{24,8},{25... | collective-permute-start | bytes 49160 | tf_op jit(solution)/shard_map/ppermute | solution.py:31
  361.6 4.9 collective-permute-start.60
  368.5 6.0 %collective-permute-start.62 = (f32[64,10,10,1]{0,3,2,1:T(1,128)S(1)}, f32[64,10,10,1]{0,3,2,1:T(1,128)S(1)}, u32[]{:S(2)}, u32[]{:S(2)}) collective-permute-start(f32[64,10,10,1]{0,3,2,1:T(1,128)S(1)} %get-tuple-element.38), channel_id=1, source_target_pairs={{1,0},{2,1},{3,2},{5,4},{6,5},{7,6},{9,8},{10,9},{11,10},{13,12},{... | collective-permute-start | bytes 76808 | tf_op jit(solution)/shard_map/ppermute | solution.py:31
  381.3 6.1 %collective-permute-start.64 = (f32[64,1,8,8]{0,3,2,1:T(8,128)S(1)}, f32[64,1,8,8]{0,3,2,1:T(8,128)S(1)}, u32[]{:S(2)}, u32[]{:S(2)}) collective-permute-start(f32[64,1,8,8]{0,3,2,1:T(8,128)S(1)} %get-tuple-element.118), channel_id=1, source_target_pairs={{16,0},{17,1},{18,2},{19,3},{20,4},{21,5},{22,6},{23,7},{24,8},{25... | collective-permute-start | bytes 49160 | tf_op jit(solution)/shard_map/ppermute | solution.py:31
  389.5 4.9 collective-permute-start.66
  396.4 6.0 %collective-permute-start.68 = (f32[64,10,10,1]{0,3,2,1:T(1,128)S(1)}, f32[64,10,10,1]{0,3,2,1:T(1,128)S(1)}, u32[]{:S(2)}, u32[]{:S(2)}) collective-permute-start(f32[64,10,10,1]{0,3,2,1:T(1,128)S(1)} %get-tuple-element.34), channel_id=1, source_target_pairs={{1,0},{2,1},{3,2},{5,4},{6,5},{7,6},{9,8},{10,9},{11,10},{13,12},{... | collective-permute-start | bytes 76808 | tf_op jit(solution)/shard_map/ppermute | solution.py:31
  422.7 5.8 collective-permute-start.70
  429.8 5.9 collective-permute-start.72
  439.1 5.8 collective-permute-start.74
  444.9 4.6 collective-permute-start.77
  455.9 5.5 collective-permute-start.78
  461.4 4.8 collective-permute-start.81
  471.9 5.5 collective-permute-start.82
  477.4 4.3 collective-permute-start.85
  487.6 5.5 collective-permute-start.86
  493.1 4.3 collective-permute-start.89
  504.2 5.8 collective-permute-start.90
  510.0 4.3 collective-permute-start.93
  520.4 5.8 collective-permute-start.94
  526.3 4.6 collective-permute-start.97
  538.0 5.8 collective-permute-start.98
  543.8 4.6 collective-permute-start.101
  552.5 6.0 %collective-permute-start.102 = (f32[64,10,10,1]{0,3,2,1:T(1,128)S(1)}, f32[64,10,10,1]{0,3,2,1:T(1,128)S(1)}, u32[]{:S(2)}, u32[]{:S(2)}) collective-permute-start(f32[64,10,10,1]{0,3,2,1:T(1,128)S(1)} %get-tuple-element.30), channel_id=1, source_target_pairs={{1,0},{2,1},{3,2},{5,4},{6,5},{7,6},{9,8},{10,9},{11,10},{13,12},{... | collective-permute-start | bytes 76808 | tf_op jit(solution)/shard_map/ppermute | solution.py:31
  565.3 5.8 collective-permute-start.104
  571.1 4.9 collective-permute-start.107
  573.2 5.1 collective-permute-start.106
  578.4 5.5 collective-permute-start.109
  582.1 6.0 %collective-permute-start.108 = (f32[64,10,10,1]{0,3,2,1:T(1,128)S(1)}, f32[64,10,10,1]{0,3,2,1:T(1,128)S(1)}, u32[]{:S(2)}, u32[]{:S(2)}) collective-permute-start(f32[64,10,10,1]{0,3,2,1:T(1,128)S(1)} %get-tuple-element.26), channel_id=1, source_target_pairs={{1,0},{2,1},{3,2},{5,4},{6,5},{7,6},{9,8},{10,9},{11,10},{13,12},{... | collective-permute-start | bytes 76808 | tf_op jit(solution)/shard_map/ppermute | solution.py:31
  (66 other events, 315.5 us)
where the time goes:
time: 605 us; the launch traced here: 594 us
  waiting for transfers between devices  210 us (35%)
  starting transfers between devices  194 us (32%)
  other arithmetic  64.5 us (11%)
  blocking collectives  53.7 us (9%)
  matrix products  37.8 us (6%)
  local copies, waits for them, and re-layouts  30 us (5%)
    ppermute x55, waiting for transfers between devices, padded_2(): after = lax.ppermute(first, axis, down)  203 us
    ppermute x55, starting transfers between devices, padded_2(): before = lax.ppermute(last, axis, up)  122 us
    ppermute x55, starting transfers between devices, padded_2(): after = lax.ppermute(first, axis, down)  72.2 us
    dot_general x47, matrix products, choose_blocks(): jnp.dot(weights, columns, precision=highest, preferred_element_type=jnp.f...  30.9 us
    all_gather x2, blocking collectives, per_device(): lax.all_gather(restrict(residual, prolong), 'gz', axis=3, tiled=True)  26.9 us
    another operation x12, other arithmetic, inverse_blocks(): factor = jnp.linalg.cholesky(diag_blocks[material])  26.1 us
    another operation x8, other arithmetic, inverse_blocks(): result.append(jax.scipy.linalg.cho_solve((factor, True), identity))  22.2 us
    concatenate x23, local copies, waits for them, and re-layouts, operate(): jnp.concatenate([centre, padded[:, 2:, 1:-1, 1:-1], padded[:, :-2, 1:-1,...  16.6 us
  transfers between devices with their start and end apart: 110, of which 76 were waited for; matrix products, arithmetic and copies ran while one was open for 1% of the time, Pallas kernels for 0%

commit v1 on v0

--- a/solution.py
+++ b/solution.py
@@ -3,6 +3,8 @@
 import jax
 import jax.numpy as jnp
 from jax import lax
+from jax.experimental import pallas as pl
+from jax.experimental.pallas import tpu as pltpu
 from jax.sharding import PartitionSpec as P
 
 MODES = 64
@@ -183,6 +185,601 @@
     return iterate.reshape(MODES, CX * CY * CZ)[None, None, None]
 
 
+HALO = 3 * SWEEPS + SWEEPS - 1
+PITCH = CY + 2 * HALO
+BLOCK = CX * CY * CZ
+TILE = 128
+LANES = -(-(PITCH * PITCH) // TILE) * TILE
+ROWS = MODES + 8
+MX, MY, MZ = CX // 2, CY // 2, CZ // 2
+VMEM_LIMIT = 48 * 1024 * 1024
+f32 = jnp.float32
+bf16 = jnp.bfloat16
+
+
+def split(value):
+    high = value.astype(bf16)
+    return high, (value - high.astype(f32)).astype(bf16)
+
+
+def dot(a, b):
+    return jnp.dot(a, b, preferred_element_type=f32)
+
+
+def iota(shape, dim):
+    return lax.broadcasted_iota(jnp.int32, shape, dim)
+
+
+def where_equal(rows, columns):
+    return jnp.where(rows == columns, 1.0, 0.0).astype(bf16)
+
+
+def place(value, selector):
+    high, low = split(value)
+    return dot(high, selector) + dot(low, selector)
+
+
+def pick(product, code, first):
+    out = jnp.zeros((MODES, product.shape[1]), f32)
+    for m in range(MATERIALS):
+        out = jnp.where(code == m + first, product[m * MODES:(m + 1) * MODES], out)
+    return out
+
+
+def stack3(value):
+    high, low = split(value)
+    return jnp.concatenate([high, low, high], axis=0)
+
+
+def halves(value):
+    high, low = split(value)
+    return jnp.concatenate([high, low], axis=0)
+
+
+def thirds(value):
+    high, low = split(value)
+    return jnp.concatenate([high, high, low], axis=1)
+
+
+def setup_kernel(diag, face, prolong, w1g, w2g, w1a, w2a, wi, wr, wp):
+    a = diag[...]
+    row_id = iota((1, MODES, 1), 1)
+    lane_id = iota((1, 1, MODES), 2)
+    for k in range(MODES):
+        pivot = 1.0 / a[:, k:k + 1, k:k + 1]
+        on_row, on_lane = row_id == k, lane_id == k
+        row = jnp.where(on_lane, pivot, a[:, k:k + 1, :] * pivot)
+        column = a[:, :, k:k + 1]
+        a = jnp.where(on_row, row, jnp.where(on_lane, 0.0, a) - column * row)
+    scaled = relax_weight * a
+    near, far, near_g, far_g, inv = [], [], [], [], []
+    zero = jnp.zeros((MODES, MODES), f32)
+    for m in range(MATERIALS):
+        beside = jnp.concatenate([face[1, m], face[0, m]], axis=1)
+        across = jnp.concatenate([face[d, m] for d in (2, 3, 4, 5)], axis=1)
+        near.append(jnp.concatenate([face[1, m], diag[m], face[0, m]], axis=1))
+        far.append(across)
+        g = jnp.dot(
+            scaled[m], jnp.concatenate([beside, across], axis=1),
+            precision=highest, preferred_element_type=f32,
+        )
+        near_g.append(jnp.concatenate([g[:, :MODES], zero, g[:, MODES:2 * MODES]], axis=1))
+        far_g.append(g[:, 2 * MODES:])
+        inv.append(scaled[m])
+    w1a[...] = halves(jnp.concatenate(near, axis=0))
+    w2a[...] = halves(jnp.concatenate(far, axis=0))
+    w1g[...] = halves(jnp.concatenate(near_g, axis=0))
+    w2g[...] = halves(jnp.concatenate(far_g, axis=0))
+    wi[...] = thirds(jnp.concatenate(inv, axis=0))
+    for p in range(2):
+        wr[p] = thirds(jnp.concatenate([restrict_scale * prolong[p * 4 + c].T for c in range(4)], axis=0))
+    wp[...] = thirds(jnp.concatenate([prolong[c] for c in range(8)], axis=0))
+
+
+def setup(diag_blocks, face_blocks, prolong):
+    both = 2 * MATERIALS * MODES
+    shapes = [(both, 3 * MODES), (both, 4 * MODES)] * 2
+    shapes += [(MATERIALS * MODES, 3 * MODES), (2, 4 * MODES, 3 * MODES), (8 * MODES, 3 * MODES)]
+    return pl.pallas_call(
+        setup_kernel,
+        out_shape=[jax.ShapeDtypeStruct(s, bf16) for s in shapes],
+        in_specs=[pl.BlockSpec(memory_space=pltpu.VMEM)] * 3,
+        out_specs=[pl.BlockSpec(memory_space=pltpu.VMEM)] * 7,
+        compiler_params=pltpu.CompilerParams(vmem_limit_bytes=VMEM_LIMIT),
+    )(diag_blocks, face_blocks, prolong)
+
+
+def layer_start(depth):
+    return sum(CY + 2 * (HALO - e) for e in range(1, depth))
+
+
+def layer_of(index):
+    depth, start = jnp.ones_like(index), jnp.zeros_like(index)
+    for d in range(2, HALO + 1):
+        inside = index >= layer_start(d)
+        depth = jnp.where(inside, d, depth)
+        start = jnp.where(inside, layer_start(d), start)
+    return depth, index - start - (HALO - depth)
+
+
+def pack_kernel(own, before, after, up, down):
+    column = iota((1, 2 * TILE), 1)
+    index = column % TILE
+    depth, y = layer_of(index)
+    z = jnp.where(column < TILE, CZ - depth, depth - 1)
+    source = ((y + CY) // CY) * TILE + ((y + CY) % CY) * CZ + z
+    source = jnp.where(index < layer_start(HALO + 1), source, -TILE)
+    row = iota((3 * TILE, 2 * TILE), 0)
+    for odd in range(2):
+        selector = where_equal(row, source + odd * CY * CZ)
+        parts = []
+        for pair in range(CX):
+            h, lane = divmod(pair * TILE, BLOCK)
+            parts.append(jnp.concatenate([r[h, :, lane:lane + TILE] for r in (before, own, after)], axis=1))
+        packed = place(jnp.concatenate(parts, axis=0), selector)
+        for pair in range(CX):
+            rows = packed[pair * ROWS:(pair + 1) * ROWS]
+            up[2 * pair + odd] = rows[:, :TILE]
+            down[2 * pair + odd] = rows[:, TILE:]
+
+
+def pack(own, before, after):
+    shape = jax.ShapeDtypeStruct((2 * CX, ROWS, TILE), f32)
+    return pl.pallas_call(
+        pack_kernel,
+        out_shape=[shape, shape],
+        in_specs=[pl.BlockSpec(memory_space=pltpu.VMEM)] * 3,
+        out_specs=[pl.BlockSpec(memory_space=pltpu.VMEM)] * 2,
+        compiler_params=pltpu.CompilerParams(vmem_limit_bytes=VMEM_LIMIT),
+    )(own, before, after)
+
+
+def fine_place(lane):
+    y = (lane * 2979) >> 16
+    return y - HALO, lane - y * PITCH - HALO
+
+
+def unpack(own, before, after, low, high, put):
+    lane = iota((1, LANES), 1)
+    y, z = fine_place(lane)
+    valid = lane < PITCH * PITCH
+    inner = ((y + CY) // CY) * TILE + ((y + CY) % CY) * CZ + z
+    depth = jnp.where(z < 0, -z, z - (CZ - 1))
+    start = jnp.zeros_like(lane)
+    for d in range(2, HALO + 1):
+        start = jnp.where(depth == d, layer_start(d), start)
+    inside = (y >= depth - HALO) & (y < CY + HALO - depth)
+    outer = jnp.where(z < 0, 3 * TILE, 4 * TILE) + start + y + HALO - depth
+    outer = jnp.where(inside, outer, -TILE)
+    middle = (z >= 0) & (z < CZ)
+    row = iota((5 * TILE, LANES), 0)
+    for odd in range(2):
+        source = jnp.where(middle, inner + odd * CY * CZ, outer)
+        selector = where_equal(row, jnp.where(valid, source, -TILE))
+        parts = []
+        for pair in range(CX):
+            h, at = divmod(pair * TILE, BLOCK)
+            x = 2 * pair + odd
+            parts.append(
+                jnp.concatenate(
+                    [r[h, :, at:at + TILE] for r in (before, own, after)] + [low[x], high[x]], axis=1
+                )
+            )
+        placed = place(jnp.concatenate(parts, axis=0), selector)
+        for pair in range(CX):
+            rows = placed[pair * ROWS:(pair + 1) * ROWS]
+            put(2 * pair + odd, rows[:MODES], rows[MODES:MODES + 1])
+
+
+class Field:
+    def __init__(self, full, high, low, shifts, masks):
+        self.full, self.high, self.low = full, high, low
+        self.shifts, self.masks = shifts, masks
+
+    def put(self, x, value):
+        self.full[x + 1] = value
+        self.high[x + 1], self.low[x + 1] = split(value)
+
+    def clear_ends(self):
+        planes = self.full.shape[0]
+        for x in (0, planes - 1):
+            self.full[x] = jnp.zeros(self.full.shape[1:], f32)
+            self.high[x] = jnp.zeros(self.full.shape[1:], bf16)
+            self.low[x] = jnp.zeros(self.full.shape[1:], bf16)
+
+    def get(self, x):
+        return self.full[x + 1]
+
+
+def field_scratch(planes, lanes):
+    shape = (planes + 2, MODES, lanes)
+    return [pltpu.VMEM(shape, f32), pltpu.VMEM(shape, bf16), pltpu.VMEM(shape, bf16)]
+
+
+def grid_neighbours(lanes, size_y, size_z, used):
+    lane = iota((1, lanes), 1)
+    y, z = lane // size_z, lane % size_z
+    inside = lane < used
+    shifts = (lanes - size_z, size_z, lanes - 1, 1)
+    masks = ((y < size_y - 1) & inside, (y > 0) & inside, (z < size_z - 1) & inside, (z > 0) & inside)
+    return shifts, masks
+
+
+def operate_plane(field, x, w1, w2, code):
+    centre = field.get(x)
+    moved = []
+    for shift, mask in zip(field.shifts, field.masks):
+        part = pltpu.roll(centre, shift, 1)
+        moved.append(part if mask is None else jnp.where(mask, part, 0.0))
+    moved_high, moved_low = split(jnp.concatenate(moved, axis=0))
+    lanes = centre.shape[1]
+    near_high = field.high[pl.ds(x, 3)].reshape(3 * MODES, lanes)
+    near_low = field.low[pl.ds(x, 3)].reshape(3 * MODES, lanes)
+    half = MATERIALS * MODES
+    wide = dot(w1[...], near_high) + dot(w2[...], moved_high)
+    total = wide[:half] + wide[half:] + dot(w1[:half], near_low) + dot(w2[:half], moved_low)
+    return centre, pick(total, code, 1)
+
+
+def planes_loop(start, count, body):
+    def pair(i, carry):
+        body(start + 2 * i)
+        body(start + 2 * i + 1)
+        return carry
+
+    lax.fori_loop(0, count // 2, pair, 0)
+    if count % 2:
+        body(start + count - 1)
+
+
+def sweep(source, target, start, count, w1, w2, gain, code):
+    def body(x):
+        centre, coupled = operate_plane(source, x, w1, w2, code[x])
+        target.put(x, (1.0 - relax_weight) * centre + gain[x] - coupled)
+
+    planes_loop(start, count, body)
+
+
+def restrict_plane(wr, residuals, parity):
+    out = 0.0
+    for p in range(2):
+        out = out + pick(dot(wr[p], stack3(residuals[p])), parity, 0)
+    return out
+
+
+def expand_planes(wp, raised_high, raised_low, parity):
+    product = dot(wp[...], jnp.concatenate([raised_high, raised_low, raised_high], axis=0))
+    return [pick(product[p * 4 * MODES:(p + 1) * 4 * MODES], parity, 0) for p in range(2)]
+
+
+def gather_mid(gathered, sizes, put):
+    n_gx, n_gy, n_gz = sizes
+    per = MX * MY * MZ
+    lines = MY * n_gz * MZ
+    column = iota((1, n_gz * 2 * per), 1)
+    k, rest = column % MZ, column // MZ
+    gz, rest = rest % n_gz, rest // n_gz
+    j, rest = rest % MY, rest // MY
+    i, h = rest % MX, rest // MX
+    source = gz * 2 * per + h * per + (i * MY + j) * MZ + k
+    selector = where_equal(iota((n_gz * 2 * per, n_gz * 2 * per), 0), source)
+    rows = gathered.shape[1]
+    parts = []
+    for block in range(n_gx * n_gy):
+        parts.append(jnp.concatenate([gathered[block * n_gz + gz] for gz in range(n_gz)], axis=1))
+    placed = place(jnp.concatenate(parts, axis=0), selector)
+    lower = iota((1, TILE), 1) < lines
+    for gx in range(n_gx):
+        for i in range(MX):
+            quarters = []
+            for h in range(2):
+                tiles = []
+                for pair in range(n_gy // 2):
+                    block = [placed[(gx * n_gy + 2 * pair + s) * rows:][:rows] for s in range(2)]
+                    at = ((h * MX + i) * lines) // TILE * TILE
+                    block = [b[:, at:at + TILE] for b in block]
+                    if i % 2 == 0:
+                        block[1] = pltpu.roll(block[1], lines, 1)
+                    else:
+                        block[0] = pltpu.roll(block[0], lines, 1)
+                    tiles.append(jnp.where(lower, block[0], block[1]))
+                quarters.append(jnp.concatenate(tiles, axis=1))
+            put(gx * MX + i, quarters)
+
+
+def solve_mid(source, gains, codes, fields, coarse, weights, grid):
+    w1g, w2g, w1a, w2a, wi, wr, wp = weights
+    planes, size_y, size_z = grid
+    lanes = size_y * size_z
+    gain, coarse_gain = gains
+    code, coarse_code = codes
+    first, second = fields
+    coarse_source, coarse_fields = coarse
+    for field in fields + coarse_fields:
+        field.clear_ends()
+
+    def start_mid(x):
+        value = pick(dot(wi[...], stack3(source[x])), code[x], 1)
+        gain[x] = value
+        first.put(x, value)
+
+    planes_loop(0, planes, start_mid)
+    sweep(first, second, 0, planes, w1g, w2g, gain, code)
+    lane = iota((1, lanes), 1)
+    y, z = lane // size_z, lane % size_z
+    parity = (y % 2) * 2 + z % 2
+    tall, wide = iota((lanes, TILE), 0), iota((lanes, TILE), 1)
+    squeeze = where_equal((tall // size_z // 2) * (size_z // 2) + tall % size_z // 2, wide)
+    target = (y // 2) * (size_z // 2) + z // 2
+    raise_lanes = where_equal(iota((TILE, lanes), 0), target)
+
+    def down(x):
+        residuals = []
+        for p in range(2):
+            unused, applied = operate_plane(second, 2 * x + p, w1a, w2a, code[2 * x + p])
+            residuals.append(source[2 * x + p] - applied)
+        coarse_value = place(restrict_plane(wr, residuals, parity), squeeze)
+        value = pick(dot(wi[...], stack3(coarse_value)), coarse_code[x], 1)
+        coarse_gain[x] = value
+        coarse_fields[0].put(x, value)
+
+    lax.fori_loop(0, planes // 2, lambda i, c: (down(i), c)[1], 0)
+    now = 0
+    for repeat in range(COARSE_SWEEPS - 1):
+        sweep(coarse_fields[now], coarse_fields[1 - now], 0, planes // 2, w1g, w2g, coarse_gain, coarse_code)
+        now = 1 - now
+    result = coarse_fields[now]
+
+    def up(x):
+        high = dot(result.high[x + 1], raise_lanes).astype(bf16)
+        low = dot(result.low[x + 1], raise_lanes).astype(bf16)
+        for p, value in enumerate(expand_planes(wp, high, low, parity)):
+            second.put(2 * x + p, second.get(2 * x + p) + value)
+
+    lax.fori_loop(0, planes // 2, lambda i, c: (up(i), c)[1], 0)
+    now = second
+    for repeat in range(SWEEPS):
+        other = first if now is second else second
+        sweep(now, other, 0, planes, w1g, w2g, gain, code)
+        now = other
+    return now
+
+
+def add_mid(place_ref, result, field, depth, wp, grid, old):
+    planes, size_y, size_z = grid
+    gx, gy, gz = place_ref[0], place_ref[1], place_ref[2]
+    lane = iota((1, LANES), 1)
+    y, z = fine_place(lane)
+    parity = (y & 1) * 2 + (z & 1)
+    whole_y, whole_z = y + gy * CY, z + gz * CZ
+    inside = (lane < PITCH * PITCH) & (whole_y >= 0) & (whole_y < 2 * size_y) & (whole_z >= 0) & (whole_z < 2 * size_z)
+    target = jnp.where(inside, (whole_y >> 1) * size_z + (whole_z >> 1), -1)
+    raise_lanes = where_equal(iota((size_y * size_z, LANES), 0), target)
+    start = gx * ((CX - depth) // 2)
+
+    def up(i, carry):
+        x = start + i
+        high = dot(result.high[x + 1], raise_lanes).astype(bf16)
+        low = dot(result.low[x + 1], raise_lanes).astype(bf16)
+        for p, value in enumerate(expand_planes(wp, high, low, parity)):
+            field.put(2 * x + p, old[2 * x + p] + value)
+        return carry
+
+    lax.fori_loop(0, (CX + depth) // 2, up, 0)
+
+
+def fine_residual(field, own, source, wr, w1a, w2a, code):
+    lane = iota((1, LANES), 1)
+    y, z = fine_place(lane)
+    parity = (y & 1) * 2 + (z & 1)
+    tall, wide = iota((LANES, TILE), 0), iota((LANES, TILE), 1)
+    y, z = fine_place(tall)
+    inside = (tall < PITCH * PITCH) & (y >= 0) & (y < CY) & (z >= 0) & (z < CZ)
+    target = jnp.where(inside, (y >> 1) * MZ + (z >> 1), -BLOCK)
+    per = MX * MY * MZ
+    index = wide % per
+    total = jnp.zeros((MODES, TILE), f32)
+    for i in range(MX):
+        residuals = []
+        for p in range(2):
+            x = own + 2 * i + p
+            unused, applied = operate_plane(field, x, w1a, w2a, code[x])
+            residuals.append(source[2 * i + p] - applied)
+        squeeze = where_equal(target + i * MY * MZ, index)
+        total = total + place(restrict_plane(wr, residuals, parity), squeeze)
+    half = MODES // 2
+    return jnp.where(iota((1, TILE), 1) < per, total[:half], total[half:])
+
+
+def fine_shifts():
+    return (LANES - PITCH, PITCH, LANES - 1, 1), (None,) * 4
+
+
+def first_kernel(grid, place_ref, own, before, after, low, high, w1g, w2g, w1a, w2a, wi, wr, wp,
+                 gain, code, solved, source, payload, a0, a1, a2, b0, b1, b2, whole):
+    first = Field(a0, a1, a2, *fine_shifts())
+    second = Field(b0, b1, b2, *fine_shifts())
+    first.clear_ends()
+    second.clear_ends()
+    gx = place_ref[0]
+
+    def put(x, value, material):
+        whole[x] = value
+        code[x] = material
+
+    unpack(own, before, after, low, high, put)
+
+    def begin(x):
+        value = pick(dot(wi[...], stack3(whole[x])), code[x], 1)
+        gain[x] = value
+        first.put(x, value)
+
+    planes_loop(0, 2 * CX, begin)
+    depth = HALO - 1
+    sweep(first, second, gx * (CX - depth), CX + depth, w1g, w2g, gain, code)
+    solved[...] = second.full[1:1 + 2 * CX]
+    mine = gx * CX
+    source[...] = whole[pl.ds(mine, CX)]
+    payload[...] = fine_residual(second, mine, source, wr, w1a, w2a, code)
+
+
+def mid_scratch(grid):
+    planes, size_y, size_z = grid
+    lanes = size_y * size_z
+    return (
+        field_scratch(planes, lanes) * 2
+        + field_scratch(planes // 2, TILE) * 2
+        + [
+            pltpu.VMEM((planes, MODES, lanes), f32),
+            pltpu.VMEM((planes, MODES, lanes), f32),
+            pltpu.VMEM((planes // 2, MODES, TILE), f32),
+            pltpu.VMEM((planes // 2, MODES, TILE), f32),
+        ]
+    )
+
+
+def run_mid(gathered, sizes, grid, weights, scratch, mid_code, coarse_code, read_codes):
+    planes, size_y, size_z = grid
+    lanes = size_y * size_z
+    near = grid_neighbours(lanes, size_y, size_z, lanes)
+    coarse_near = grid_neighbours(TILE, size_y // 2, size_z // 2, lanes // 4)
+    fields = [Field(*scratch[0:3], *near), Field(*scratch[3:6], *near)]
+    coarse_fields = [Field(*scratch[6:9], *coarse_near), Field(*scratch[9:12], *coarse_near)]
+    source, gain, coarse_source, coarse_gain = scratch[12:16]
+    half = MODES // 2
+    tall, wide = iota((lanes, TILE), 0), iota((lanes, TILE), 1)
+    y, z = tall // size_z, tall % size_z
+    corner = jnp.where((y % 2 == 0) & (z % 2 == 0), (y // 2) * (size_z // 2) + z // 2, -1)
+
+    def put(x, quarters):
+        source[x, :half] = quarters[0][:half]
+        source[x, half:] = quarters[1][:half]
+        if read_codes:
+            mid_code[x] = quarters[0][half:half + 1]
+            if x % 2 == 0:
+                rows = jnp.broadcast_to(quarters[1][half:half + 1], (8, lanes)).astype(bf16)
+                coarse_code[x // 2] = dot(rows, where_equal(corner, wide))[:1]
+
+    gather_mid(gathered, sizes, put)
+    return solve_mid(
+        source, (gain, coarse_gain), (mid_code, coarse_code), fields, (coarse_source, coarse_fields), weights, grid
+    )
+
+
+def second_kernel(sizes, grid, place_ref, gathered, gain, code, solved, source, w1g, w2g, w1a, w2a, wi, wr, wp,
+                  payload, result, mid_code, coarse_code, a0, a1, a2, b0, b1, b2, *scratch):
+    weights = (w1g, w2g, w1a, w2a, wi, wr, wp)
+    answer = run_mid(gathered, sizes, grid, weights, scratch, mid_code, coarse_code, True)
+    now, other = Field(a0, a1, a2, *fine_shifts()), Field(b0, b1, b2, *fine_shifts())
+    now.clear_ends()
+    other.clear_ends()
+    depth = 3 * SWEEPS
+    gx = place_ref[0]
+    add_mid(place_ref, answer, now, depth, wp, grid, solved)
+    for repeat in range(2 * SWEEPS):
+        depth -= 1
+        sweep(now, other, gx * (CX - depth), CX + depth, w1g, w2g, gain, code)
+        now, other = other, now
+    payload[...] = fine_residual(now, gx * CX, source, wr, w1a, w2a, code)
+    result[...] = now.full[1:1 + 2 * CX]
+
+
+def third_kernel(sizes, grid, place_ref, gathered, mid_code, coarse_code, gain, code, solved,
+                 w1g, w2g, w1a, w2a, wi, wr, wp, result, a0, a1, a2, b0, b1, b2, *scratch):
+    weights = (w1g, w2g, w1a, w2a, wi, wr, wp)
+    answer = run_mid(gathered, sizes, grid, weights, scratch, mid_code, coarse_code, False)
+    now, other = Field(a0, a1, a2, *fine_shifts()), Field(b0, b1, b2, *fine_shifts())
+    now.clear_ends()
+    other.clear_ends()
+    depth = SWEEPS
+    gx = place_ref[0]
+    add_mid(place_ref, answer, now, depth, wp, grid, solved)
+    for repeat in range(SWEEPS):
+        depth -= 1
+        sweep(now, other, gx * (CX - depth), CX + depth, w1g, w2g, gain, code)
+        now, other = other, now
+    tall, wide = iota((LANES, TILE), 0), iota((LANES, TILE), 1)
+    y, z = fine_place(tall)
+    inside = (tall < PITCH * PITCH) & (y >= 0) & (y < CY) & (z >= 0) & (z < CZ)
+    target = jnp.where(inside, y * CZ + z, -BLOCK)
+    selectors = [where_equal(target + odd * CY * CZ, wide) for odd in range(2)]
+    for pair in range(CX // 2):
+        total = 0.0
+        for odd in range(2):
+            value = now.get(gx * CX + 2 * pair + odd)
+            high, low = split(value)
+            lowest = (value - high.astype(f32) - low.astype(f32)).astype(bf16)
+            for part in (high, low, lowest):
+                total = total + dot(part, selectors[odd])
+        result[:, pair * TILE:(pair + 1) * TILE] = total
+
+
+def call(kernel, out_shape, scratch, *args):
+    vmem = pl.BlockSpec(memory_space=pltpu.VMEM)
+    return pl.pallas_call(
+        kernel,
+        out_shape=out_shape,
+        in_specs=[pl.BlockSpec(memory_space=pltpu.SMEM)] + [vmem] * (len(args) - 1),
+        out_specs=jax.tree.map(lambda s: vmem, out_shape),
+        scratch_shapes=scratch,
+        compiler_params=pltpu.CompilerParams(vmem_limit_bytes=VMEM_LIMIT),
+    )(*args)
+
+
+def shape_of(*dims):
+    return jax.ShapeDtypeStruct(dims, f32)
+
+
+def wide_device(sizes, right_side, diag_blocks, face_blocks, prolong, mats_fine, mats_mid, mats_coarse):
+    n_gx, n_gy, n_gz = sizes
+    axes = ("gx", "gy", "gz")
+    grid = (n_gx * MX, n_gy * MY, n_gz * MZ)
+    place_ref = jnp.stack([lax.axis_index(a) for a in axes]).astype(jnp.int32)
+    codes = (mats_fine.reshape(1, BLOCK) + 1).astype(f32)
+    block = jnp.concatenate([right_side.reshape(MODES, BLOCK), jnp.broadcast_to(codes, (8, BLOCK))], axis=0)
+    other = lax.ppermute(block, "gx", [(0, 1), (1, 0)])
+    own = jnp.where(place_ref[0] == 0, jnp.stack([block, other]), jnp.stack([other, block]))
+    up = {a: [(i, i + 1) for i in range(n - 1)] for a, n in zip(axes, sizes)}
+    down = {a: [(j, i) for i, j in pairs] for a, pairs in up.items()}
+    before, after = lax.ppermute(own, "gy", up["gy"]), lax.ppermute(own, "gy", down["gy"])
+    send_up, send_down = pack(own, before, after)
+    low, high = lax.ppermute(send_up, "gz", up["gz"]), lax.ppermute(send_down, "gz", down["gz"])
+    weights = setup(diag_blocks, face_blocks, prolong)
+
+    fine = field_scratch(2 * CX, LANES) * 2
+    half, per = MODES // 2, MX * MY * MZ
+    whole = shape_of(2 * CX, MODES, LANES)
+    gain, code, solved, source, payload = call(
+        partial(first_kernel, grid),
+        [whole, shape_of(2 * CX, 1, LANES), whole, shape_of(CX, MODES, LANES), shape_of(half, TILE)],
+        fine + [pltpu.VMEM((2 * CX, MODES, LANES), f32)],
+        place_ref, own, before, after, low, high, *weights,
+    )
+    mid = (mats_mid.reshape(per) + 1).astype(f32)
+    coarse = (mats_coarse.reshape(MX // 2, 1, MY // 2, 1, MZ // 2, 1) + 1).astype(f32)
+    coarse = jnp.broadcast_to(coarse, (MX // 2, 2, MY // 2, 2, MZ // 2, 2)).reshape(per)
+    tail = jnp.broadcast_to(jnp.concatenate([mid, coarse])[None], (8, TILE))
+
+    def to_all(value):
+        copies = jnp.broadcast_to(value[None], (n_gx * n_gy * n_gz,) + value.shape)
+        return lax.all_to_all(copies, axes, 0, 0)
+
+    planes, lanes = grid[0], grid[1] * grid[2]
+    payload, solved, mid_code, coarse_code = call(
+        partial(second_kernel, sizes, grid),
+        [shape_of(half, TILE), whole, shape_of(planes, 1, lanes), shape_of(planes // 2, 1, TILE)],
+        fine + mid_scratch(grid),
+        place_ref, to_all(jnp.concatenate([payload, tail], axis=0)), gain, code, solved, source, *weights,
+    )
+    result = call(
+        partial(third_kernel, sizes, grid),
+        shape_of(MODES, BLOCK),
+        fine + mid_scratch(grid),
+        place_ref, to_all(payload), mid_code, coarse_code, gain, code, solved, *weights,
+    )
+    return result[None, None, None]
+
+
 def solution(mesh):
     placed = (
         P("gx", "gy", "gz", None, None),
@@ -193,8 +790,10 @@
         P("gx", "gy", "gz", None),
         P("gx", "gy", "gz", None),
     )
+    sizes = tuple(mesh.shape[a] for a in ("gx", "gy", "gz"))
+    wide = sizes[0] == 2 and sizes[1] % 2 == 0 and sizes[2] * MY * MZ * 2 == TILE and sizes[1] <= 4
     return jax.shard_map(
-        per_device,
+        partial(wide_device, sizes) if wide else per_device,
         mesh=mesh,
         in_specs=placed,
         out_specs=P("gx", "gy", "gz", None, None),

time: 605 us -> 197 us (0.33); the launches traced: 594 us -> 196 us
  waiting for transfers between devices: 210 us -> 11.7 us
  starting transfers between devices: 194 us -> 12.4 us
  Pallas kernels: 0 us -> 126 us
  other arithmetic: 64.5 us -> 2.56 us
  matrix products: 37.8 us -> 0 us
  local copies, waits for them, and re-layouts: 30 us -> 1.7 us
  blocking collectives: 53.7 us -> 41.5 us
    ppermute x110 -> x5, waiting for transfers between devices: 210 us -> 11.7 us  [the longest x1 4.6 us: wide_device(): lax.ppermute(send_down, 'gz', down['gz'])]
    ppermute x110 -> x5, starting transfers between devices: 194 us -> 12.4 us  [the longest x1 3.72 us: wide_device(): lax.ppermute(send_up, 'gz', up['gz'])]
    pallas_call x0 -> x5, Pallas kernels: none -> 126 us  [the longest x3 118 us: call(): pl.pallas_call(kernel, out_shape=out_shape, in_specs=[pl.BlockSpec(memory...]
    all_gather x4 -> x0, blocking collectives: 53.7 us -> none  [the longest x2 26.9 us: per_device(): lax.all_gather(restrict(residual, prolong), 'gz', axis=3, tiled=True)]
    another operation x20 -> x2, other arithmetic: 48.3 us -> 1 us  [the longest x1 0.92 us: wide_device(): jnp.stack([block, other])]
    all_to_all x0 -> x2, blocking collectives: none -> 41.5 us  [to_all(): return lax.all_to_all(copies, axes, 0, 0)]
    dot_general x55 -> x0, matrix products: 36.2 us -> none  [the longest x47 30.9 us: choose_blocks(): jnp.dot(weights, columns, precision=highest, preferred_element_type=jnp.f...]
    concatenate x23 -> x0, local copies, waits for them, and re-layouts: 16.6 us -> none  [operate(): jnp.concatenate([centre, padded[:, 2:, 1:-1, 1:-1], padded[:, :-2, 1:-1,...]
  transfers between devices with their start and end apart: 110 -> 5, of which waited for: 76 -> 4; matrix products, arithmetic and copies ran while one was open for 1% -> 1% of each run, Pallas kernels for 0% -> 3%
where the time goes in v1:
time: 197 us; the launch traced here: 196 us
  Pallas kernels  126 us (64%)
  blocking collectives  41.5 us (21%)
  starting transfers between devices  12.4 us (6%)
  waiting for transfers between devices  11.7 us (6%)
  other arithmetic  2.56 us (1%)
    pallas_call x3, Pallas kernels, call(): pl.pallas_call(kernel, out_shape=out_shape, in_specs=[pl.BlockSpec(memory...  118 us
    all_to_all x2, blocking collectives, to_all(): return lax.all_to_all(copies, axes, 0, 0)  41.5 us
    pallas_call x1, Pallas kernels, setup(): pl.pallas_call(setup_kernel, out_shape=[jax.ShapeDtypeStruct(s, bf16) for...  6.76 us
    ppermute x1, waiting for transfers between devices, wide_device(): lax.ppermute(send_down, 'gz', down['gz'])  4.6 us
  transfers between devices with their start and end apart: 5, of which 4 were waited for; matrix products, arithmetic and copies ran while one was open for 1% of the time, Pallas kernels for 3%

profile of v1, /device:TPU:0, one launch (start us, length us, event | category | flops | bytes accessed | tf_op | source)
XLA Modules:
  0.0 196.5 jit_solution(14726579056485892049)
XLA Ops:
  0.0 0.0 copy-start.3
  0.0 0.0 copy-start.2
  0.0 0.0 copy-start.4
  0.0 0.0 copy-start.5
  0.0 0.8 add_convert_fusion
  0.8 0.9 fusion
  1.7 3.0 %collective-permute-start = (f32[72,512]{1,0:T(8,128)S(1)}, f32[72,512]{1,0:T(8,128)S(1)}, u32[]{:S(2)}, u32[]{:S(2)}) collective-permute-start(f32[72,512]{1,0:T(8,128)S(1)} %get-tuple-element.42), channel_id=1, source_target_pairs={{0,16},{16,0},{1,17},{17,1},{2,18},{18,2},{3,19},{19,3},{4,20},{20... | collective-permute-start | bytes 442376 | tf_op jit(solution)/shard_map/ppermute | solution.py:740
  4.8 3.8 %collective-permute-done = f32[72,512]{1,0:T(8,128)S(1)} collective-permute-done((f32[72,512]{1,0:T(8,128)S(1)}, f32[72,512]{1,0:T(8,128)S(1)}, u32[]{:S(2)}, u32[]{:S(2)}) %collective-permute-start) | collective-permute-done | bytes 147488 | tf_op jit(solution)/shard_map/ppermute | solution.py:740
  8.6 1.3 collective-permute-start.2
  9.9 3.0 %collective-permute-start.1 = (f32[2,72,512]{2,1,0:T(8,128)S(1)}, f32[2,72,512]{2,1,0:T(8,128)S(1)}, u32[]{:S(2)}, u32[]{:S(2)}) collective-permute-start(f32[2,72,512]{2,1,0:T(8,128)S(1)} %maximum_select_fusion.own), channel_id=1, source_target_pairs={{0,4},{4,8},{8,12},{1,5},{5,9},{9,13},{2,6},{6,10},{10,14},{3,7},{... | collective-permute-start | bytes 884744 | tf_op jit(solution)/shard_map/ppermute | solution.py:744
  13.0 0.0 collective-permute-done.2.after
  13.0 1.2 collective-permute-done.1.before
  14.2 1.9 shard_map.73
  16.1 3.7 %collective-permute-start.3 = (f32[16,72,128]{2,1,0:T(8,128)}, f32[16,72,128]{2,1,0:T(8,128)S(1)}, u32[]{:S(2)}, u32[]{:S(2)}) collective-permute-start(f32[16,72,128]{2,1,0:T(8,128)} %get-tuple-element.23), channel_id=1, source_target_pairs={{0,1},{1,2},{2,3},{4,5},{5,6},{6,7},{8,9},{9,10},{10,11},{12,13},{... | collective-permute-start | bytes 1769480 | tf_op jit(solution)/shard_map/ppermute | solution.py:746
  19.8 1.3 collective-permute-start.4
  21.1 0.7 convert_reduce_fusion
  21.8 0.1 convert_element_type.33
  21.9 0.1 broadcast_in_dim.13
  21.9 0.1 reshape.40
  22.0 0.0 copy-done.3
  22.1 0.0 copy-done.2
  22.1 0.0 copy-done.4
  22.1 6.8 %shard_map.74 = (bf16[512,192]{1,0:T(8,128)(2,1)S(1)}, bf16[512,256]{1,0:T(8,128)(2,1)S(1)}, bf16[512,192]{1,0:T(8,128)(2,1)S(1)}, bf16[512,256]{1,0:T(8,128)(2,...) custom-call(f32[4,64,64]{2,1,0:T(8,128)S(1)} %copy-done.4, ...), custom_call_target="tpu_custom_call" | custom-call | tf_op jit(solution)/shard_map/pallas_call | solution.py:283
  28.8 0.0 copy-done.5
  28.9 0.1 pad_maximum_fusion.2
  28.9 0.1 pad_add_fusion.place_ref
  29.0 2.1 %collective-permute-done.3.low = f32[16,72,128]{2,1,0:T(8,128)S(1)} collective-permute-done((f32[16,72,128]{2,1,0:T(8,128)}, f32[16,72,128]{2,1,0:T(8,128)S(1)}, u32[]{:S(2)}, u32[]{:S(2)}) %collective-permute-start.3) | collective-permute-done | bytes 589856 | tf_op jit(solution)/shard_map/ppermute | solution.py:746
  31.1 4.6 %collective-permute-done.4.high = f32[16,72,128]{2,1,0:T(8,128)S(1)} collective-permute-done((f32[16,72,128]{2,1,0:T(8,128)}, f32[16,72,128]{2,1,0:T(8,128)S(1)}, u32[]{:S(2)}, u32[]{:S(2)}) %collective-permute-start.4) | collective-permute-done | bytes 589856 | tf_op jit(solution)/shard_map/ppermute | solution.py:746
  35.7 20.3 %shard_map.75 = (f32[16,64,512]{2,1,0:T(8,128)}, f32[16,1,512]{2,1,0:T(1,128)S(1)}, f32[16,64,512]{2,1,0:T(8,128)}, f32[8,64,512]{2,1,0:T(8,128)S(1)}, f32[32,128]{1,0:T(8,128)S(1)}) custom-call(s32[3]{0:T(128)S(1)} %pad_add_fusion.place_ref, f32[2,72,512]{2,1,0:T(8,128)S(1)} %maximum_select_fusion.own, f32[2,72,512]{2,1,0:T(8,128)S(1)} %collective-permute-done.1.before, ...), custom_call_target="tpu_custom_call" | custom-call | tf_op jit(solution)/shard_map/pallas_call | solution.py:719
  56.1 23.0 %all_to_all.10.gathered = f32[32,40,128]{2,1,0:T(8,128)S(1)} all-to-all(f32[32,40,128]{2,1,0:T(8,128)S(1)} %broadcast_in_dim.15), channel_id=1, replica_groups=mesh['gx'=2,'gy'=4,'gz'=4] {'gx','gy','gz'}, dimensions={0} | all-to-all | bytes 1310720 | tf_op jit(solution)/shard_map/all_to_all | solution.py:765
  79.2 0.0 copy-start
  79.2 60.2 %shard_map.76 = (f32[32,128]{1,0:T(8,128)S(1)}, f32[16,64,512]{2,1,0:T(8,128)S(1)}, f32[8,1,256]{2,1,0:T(1,128)S(1)}, f32[4,1,128]{2,1,0:T(1,128)S(1)}) custom-call(s32[3]{0:T(128)S(1)} %pad_add_fusion.place_ref, f32[32,40,128]{2,1,0:T(8,128)S(1)} %all_to_all.10.gathered, f32[16,64,512]{2,1,0:T(8,128)} %get-tuple-element.33.gain, ...), custom_call_target="tpu_custom_call" | custom-call | tf_op jit(solution)/shard_map/pallas_call | solution.py:719
  139.4 0.0 copy-start.1
  139.4 1.3 copy-done.1
  140.8 18.5 %all_to_all.11.gathered = f32[32,32,128]{2,1,0:T(8,128)S(1)} all-to-all(f32[32,32,128]{2,1,0:T(8,128)S(1)} %broadcast_in_dim.16), channel_id=1, replica_groups=mesh['gx'=2,'gy'=4,'gz'=4] {'gx','gy','gz'}, dimensions={0} | all-to-all | bytes 1048576 | tf_op jit(solution)/shard_map/all_to_all | solution.py:765
  159.2 0.0 copy-done
  159.2 37.2 %shard_map.77 = f32[64,512]{1,0:T(8,128)} custom-call(s32[3]{0:T(128)S(1)} %pad_add_fusion.place_ref, f32[32,32,128]{2,1,0:T(8,128)S(1)} %all_to_all.11.gathered, f32[8,1,256]{2,1,0:T(1,128)S(1)} %get-tuple-element.38.mid_code, f32[4,1,128]{2,1,0:T(1,128)S(1)} %get-tuple-element.39.coarse_code, f32[16,64,512]{2,1,0:T(8,128)S(1)} %copy-done, ...), custom_call_target="tpu_custom_call" | custom-call | tf_op jit(solution)/shard_map/pallas_call | solution.py:719
  (7 shorter events, 0.1 us)
Async XLA Ops:
  0.0 22.1 %copy-start.3 = (f32[8,64,64]{2,1,0:T(8,128)S(1)}, f32[8,64,64]{2,1,0:T(8,128)}, u32[]{:S(2)}) copy-start(f32[8,64,64]{2,1,0:T(8,128)} %prolong.1) | copy-start | bytes 393220
  0.0 22.1 %copy-start.2 = (f32[6,4,64,64]{3,2,1,0:T(8,128)S(1)}, f32[6,4,64,64]{3,2,1,0:T(8,128)}, u32[]{:S(2)}) copy-start(f32[6,4,64,64]{3,2,1,0:T(8,128)} %face.1) | copy-start | bytes 1179652
  0.0 22.1 %copy-start.4 = (f32[4,64,64]{2,1,0:T(8,128)S(1)}, f32[4,64,64]{2,1,0:T(8,128)}, u32[]{:S(2)}) copy-start(f32[4,64,64]{2,1,0:T(8,128)} %diag.1) | copy-start | bytes 196612
  0.0 28.8 %copy-start.5 = (s32[1,1,1,64]{3,2,1,0:T(1,128)S(1)}, s32[1,1,1,64]{3,2,1,0:T(1,128)}, u32[]{:S(2)}) copy-start(s32[1,1,1,64]{3,2,1,0:T(1,128)} %param.12) | copy-start | bytes 772
  1.7 6.9 %collective-permute-start = (f32[72,512]{1,0:T(8,128)S(1)}, f32[72,512]{1,0:T(8,128)S(1)}, u32[]{:S(2)}, u32[]{:S(2)}) collective-permute-start(f32[72,512]{1,0:T(8,128)S(1)} %get-tuple-element.42), channel_id=1, source_target_pairs={{0,16},{16,0},{1,17},{17,1},{2,18},{18,2},{3,19},{19,3},{4,20},{20... | collective-permute-start | bytes 442376 | tf_op jit(solution)/shard_map/ppermute | solution.py:740
  8.6 4.4 %collective-permute-start.2 = (f32[2,72,512]{2,1,0:T(8,128)S(1)}, f32[2,72,512]{2,1,0:T(8,128)S(1)}, u32[]{:S(2)}, u32[]{:S(2)}) collective-permute-start(f32[2,72,512]{2,1,0:T(8,128)S(1)} %maximum_select_fusion.own), channel_id=1, source_target_pairs={{4,0},{8,4},{12,8},{5,1},{9,5},{13,9},{6,2},{10,6},{14,10},{7,3},{... | collective-permute-start | bytes 884744 | tf_op jit(solution)/shard_map/ppermute | solution.py:744
  9.9 4.2 %collective-permute-start.1 = (f32[2,72,512]{2,1,0:T(8,128)S(1)}, f32[2,72,512]{2,1,0:T(8,128)S(1)}, u32[]{:S(2)}, u32[]{:S(2)}) collective-permute-start(f32[2,72,512]{2,1,0:T(8,128)S(1)} %maximum_select_fusion.own), channel_id=1, source_target_pairs={{0,4},{4,8},{8,12},{1,5},{5,9},{9,13},{2,6},{6,10},{10,14},{3,7},{... | collective-permute-start | bytes 884744 | tf_op jit(solution)/shard_map/ppermute | solution.py:744
  16.1 15.1 %collective-permute-start.3 = (f32[16,72,128]{2,1,0:T(8,128)}, f32[16,72,128]{2,1,0:T(8,128)S(1)}, u32[]{:S(2)}, u32[]{:S(2)}) collective-permute-start(f32[16,72,128]{2,1,0:T(8,128)} %get-tuple-element.23), channel_id=1, source_target_pairs={{0,1},{1,2},{2,3},{4,5},{5,6},{6,7},{8,9},{9,10},{10,11},{12,13},{... | collective-permute-start | bytes 1769480 | tf_op jit(solution)/shard_map/ppermute | solution.py:746
  19.8 15.9 %collective-permute-start.4 = (f32[16,72,128]{2,1,0:T(8,128)}, f32[16,72,128]{2,1,0:T(8,128)S(1)}, u32[]{:S(2)}, u32[]{:S(2)}) collective-permute-start(f32[16,72,128]{2,1,0:T(8,128)} %get-tuple-element.24), channel_id=1, source_target_pairs={{1,0},{2,1},{3,2},{5,4},{6,5},{7,6},{9,8},{10,9},{11,10},{13,12},{... | collective-permute-start | bytes 1769480 | tf_op jit(solution)/shard_map/ppermute | solution.py:746
  79.2 80.1 %copy-start = (f32[16,64,512]{2,1,0:T(8,128)S(1)}, f32[16,64,512]{2,1,0:T(8,128)}, u32[]{:S(2)}) copy-start(f32[16,64,512]{2,1,0:T(8,128)} %get-tuple-element.33.gain) | copy-start | bytes 6291460
  139.4 1.3 copy-start.1
